TPU v7x, 32 devices: a whole 2x2x4 slice. The times are simulated.
32 devices in a mesh: rows: 16 (over z, y, core), grp: 2 (over x).
Axes of the slice: x: 2, y: 2, z: 4, core: 2. Of those that a mesh axis runs over, the one named last changes fastest.
Arguments:
- a_tiles: bfloat16 [512, 64, 1728], P(('rows', 'grp')), may hold values from -0.15625 to 0.15625
- p_tiles: bfloat16 [512, 64, 192], P(('rows', 'grp')), may hold values from -0.75 to 0.75
- acols: int32 [512, 27], P(('rows', 'grp')), may hold values from 0 to 511, as said below
- agg: int32 [512], replicated, may hold values from 0 to 63, as said below
Outputs:
- coarse_op: float32 [64, 64, 704], P(('rows', 'grp'))
Inputs may be any that keep to these rules, and one draw needn't show every extreme that they name: `acols`: the 27 block columns of row i are distinct, each (i + o) mod 512 with o in -14..14; o = 0, -14 and 14 are always among them. agg never falls; aggregate c begins at fine block row 8 * c + r_c with r_c = 0 for even c and |r_c| at most 4 for odd c, so every aggregate has 4 to 12 rows, and some aggregate has 12.
All inputs are finite; a program needn't handle non-finite values.
Results may differ from a plain program's by a relative error of at most 0.0029.
Values may be sent and summed in bfloat16 or wider, within the bound.
A program may use at most 64 MiB of HBM per device.

v0:
```python
import jax
import jax.numpy as jnp
from jax import lax
from jax.sharding import PartitionSpec as P

PCOLS = 3
RATIO = 8
REACH = 14


def with_halo(cells, sides, width):
    for axis, dim in sides:
        count = lax.axis_size(axis)
        head = lax.slice_in_dim(cells, 0, width, axis=dim)
        tail = lax.slice_in_dim(cells, cells.shape[dim] - width, cells.shape[dim], axis=dim)
        cells = jnp.concatenate(
            [
                lax.ppermute(tail, axis, [(i, (i + 1) % count) for i in range(count)]),
                cells,
                lax.ppermute(head, axis, [((i + 1) % count, i) for i in range(count)]),
            ],
            axis=dim,
        )
    return cells


def tile_bands(a_rows, picked, shifts, tile_size):
    row_count = a_rows.shape[0]
    link_count = picked.shape[1]
    blocks = a_rows.reshape(row_count, tile_size, link_count, tile_size)
    selector = (shifts[:, None, :] == jnp.arange(7, dtype=jnp.int32)[None, :, None]).astype(
        jnp.bfloat16
    )
    masked = blocks[:, None] * selector[:, :, None, :, None]
    grouped = jnp.einsum("bsrkc,bkcq->brsq", masked, picked, preferred_element_type=jnp.float32)
    split_cols = grouped.reshape(row_count, tile_size, 7, 3, tile_size)
    widened = jnp.pad(split_cols[:, :, :, 0], ((0, 0), (0, 0), (0, 2), (0, 0)))
    widened = widened + jnp.pad(split_cols[:, :, :, 1], ((0, 0), (0, 0), (1, 1), (0, 0)))
    widened = widened + jnp.pad(split_cols[:, :, :, 2], ((0, 0), (0, 0), (2, 0), (0, 0)))
    return widened.reshape(row_count, tile_size, 9 * tile_size).astype(jnp.bfloat16)


def own_bands(a_tiles, acols, own_agg, agg, p_ext, ext_start, tile_size):
    rows_dev = a_tiles.shape[0]
    total_rows = agg.shape[0]
    coarse_count = total_rows // RATIO
    block_count = rows_dev // 4
    local_rows = (acols - ext_start) % total_rows
    shifts = (jnp.take(agg, acols) - own_agg[:, None] + 3) % coarse_count

    def block_bands(pieces):
        a_piece, local_piece, shift_piece = pieces
        picked = jnp.take(p_ext, local_piece, axis=0)
        return tile_bands(a_piece, picked, shift_piece, tile_size)

    widened = lax.map(
        block_bands,
        (
            a_tiles.reshape(block_count, 4, tile_size, a_tiles.shape[2]),
            local_rows.reshape(block_count, 4, acols.shape[1]),
            shifts.reshape(block_count, 4, acols.shape[1]),
        ),
    )
    return widened.reshape(rows_dev, tile_size, 9 * tile_size)


def coarse_terms(p_rows, widened, rows_agg, window_start, window_rows, coarse_count, tile_size):
    partial_value = jnp.zeros((window_rows, tile_size, 11 * tile_size), jnp.float32)
    for column in range(PCOLS):
        p_column = p_rows[:, :, column * tile_size : (column + 1) * tile_size]
        slots = (rows_agg + column - 1 - window_start) % coarse_count
        onehot = (slots[None, :] == jnp.arange(window_rows, dtype=jnp.int32)[:, None]).astype(
            jnp.bfloat16
        )
        masked = onehot[:, :, None, None] * p_column[None]
        coarse_term = jnp.einsum(
            "wbrc,brq->wcq", masked, widened, preferred_element_type=jnp.float32
        )
        partial_value = partial_value + jnp.pad(
            coarse_term, ((0, 0), (0, 0), ((2 - column) * tile_size, column * tile_size))
        )
    return partial_value


def shards(a_tiles, p_tiles, acols, agg):
    rows_dev = a_tiles.shape[0]
    tile_size = a_tiles.shape[1]
    total_rows = agg.shape[0]
    coarse_count = total_rows // RATIO
    coarse_dev = rows_dev // RATIO
    device = lax.axis_index(("rows", "grp"))
    first_row = device * rows_dev
    own_agg = lax.dynamic_slice_in_dim(agg, first_row, rows_dev)
    margin = RATIO + RATIO // 2
    p_margin = max(REACH, margin)
    p_ext = with_halo(p_tiles, ((("rows", "grp"), 0),), p_margin)
    widened = own_bands(a_tiles, acols, own_agg, agg, p_ext, first_row - p_margin, tile_size)
    band_ext = with_halo(widened, ((("rows", "grp"), 0),), margin)
    p_window = p_ext[p_margin - margin : p_margin - margin + rows_dev + 2 * margin]
    ext_index = (
        first_row - margin + jnp.arange(rows_dev + 2 * margin, dtype=jnp.int32)
    ) % total_rows
    ext_agg = jnp.take(agg, ext_index)
    result = coarse_terms(
        p_window, band_ext, ext_agg, device * coarse_dev, coarse_dev, coarse_count, tile_size
    )
    return result


def solution(mesh):
    return jax.shard_map(
        shards,
        mesh=mesh,
        in_specs=(
            P(("rows", "grp"), None, None),
            P(("rows", "grp"), None, None),
            P(("rows", "grp"), None),
            P(),
        ),
        out_specs=P(("rows", "grp"), None, None),
        check_vma=False,
    )
```

profile of v0, /device:TPU:0, one launch (start us, length us, event | category | flops | bytes accessed | tf_op | source)
XLA Modules:
  0.0 234.7 jit_solution(1049638943260900355)
XLA Ops:
  1.2 3.0 %collective-permute-start = (bf16[14,64,192]{2,1,0:T(8,128)(2,1)S(1)}, bf16[14,64,192]{2,1,0:T(8,128)(2,1)S(1)}, u32[]{:S(2)}, u32[]{:S(2)}) collective-permute-start(bf16[14,64,192]{2,1,0:T(8,128)(2,1)S(1)} %get-tuple-element.106), channel_id=1, source_target_pairs={{0,1},{1,2},{2,3},{3,4},{4,5},{5,6},{6,7},{7,8},{8,9},{9,10},{10,1... | collective-permute-start | bytes 1032200 | tf_op jit(solution)/shard_map/ppermute | solution.py:18
  4.2 3.5 %collective-permute-start.1 = (bf16[14,64,192]{2,1,0:T(8,128)(2,1)S(1)}, bf16[14,64,192]{2,1,0:T(8,128)(2,1)S(1)}, u32[]{:S(2)}, u32[]{:S(2)}) collective-permute-start(bf16[14,64,192]{2,1,0:T(8,128)(2,1)S(1)} %get-tuple-element.105), channel_id=1, source_target_pairs={{1,0},{2,1},{3,2},{4,3},{5,4},{6,5},{7,6},{8,7},{9,8},{10,9},{11,1... | collective-permute-start | bytes 1032200 | tf_op jit(solution)/shard_map/ppermute | solution.py:20
  9.4 3.1 %gather_fusion.2 = s32[432]{0:T(512)S(1)} fusion(s32[512]{0:T(512)S(1)} %copy-done, s32[1024]{0:T(1024)S(1)} %get-tuple-element.111), kind=kCustom, calls=%fused_computation.2 | custom fusion | bytes 5184 | tf_op jit(solution)/shard_map/jit(_take)/gather | solution.py:49
  14.8 5.3 %collective-permute-done = bf16[14,64,192]{2,1,0:T(8,128)(2,1)S(1)} collective-permute-done((bf16[14,64,192]{2,1,0:T(8,128)(2,1)S(1)}, bf16[14,64,192]{2,1,0:T(8,128)(2,1)S(1)}, u32[]{:S(2)}, u32[]{:S(2)}) %collective-permute-start) | collective-permute-done | bytes 344096 | tf_op jit(solution)/shard_map/ppermute | solution.py:18
  20.2 4.4 %collective-permute-done.1 = bf16[14,64,192]{2,1,0:T(8,128)(2,1)S(1)} collective-permute-done((bf16[14,64,192]{2,1,0:T(8,128)(2,1)S(1)}, bf16[14,64,192]{2,1,0:T(8,128)(2,1)S(1)}, u32[]{:S(2)}, u32[]{:S(2)}) %collective-permute-start.1) | collective-permute-done | bytes 344096 | tf_op jit(solution)/shard_map/ppermute | solution.py:20
  24.6 149.1 %while.12 = (s32[]{:T(128)}, bf16[4,4,64,576]{2,3,1,0:T(8,128)(2,1)}, s32[4,4,27]{2,1,0:T(4,128)S(1)}, bf16[44,64,192]{2,1,0:T(8,128)(2,1)S(1)}, bf16[4,4,64,172...) while((s32[]{:T(128)}, bf16[4,4,64,576]{2,3,1,0:T(8,128)(2,1)}, s32[4,4,27]{2,1,0:T(4,128)S(1)}, ...), condition=%wide.region_1.2_spmd, body=%wide.region_0.1_spmd.sunk | while | flops 1203244416 | bytes 34222540 | solution.py:56
  24.7 2.7 %gather_fusion = bf16[108,64,192]{2,1,0:T(8,128)(2,1)} fusion(bf16[44,64,192]{2,1,0:T(8,128)(2,1)S(1)} %get-tuple-element.173, s32[1024]{0:T(1024)S(1)} %pad_clamp_fusion.4), kind=kCustom, calls=%fused_computation.clone.1 | custom fusion | bytes 5308848 | tf_op jit(solution)/shard_map/while/body/eval_jaxpr/jit(_take)/gather | solution.py:53
  30.2 3.2 %mul.147 = bf16[4,64,27,64]{3,2,1,0:T(8,128)(2,1)S(1)} reshape(bf16[1,4,64,1728]{3,2,1,0:T(8,128)(2,1)} %constant_dynamic-slice_fusion.2) | data formatting | bytes 1769472 | tf_op jit(solution)/shard_map/while/body/eval_jaxpr/mul | solution.py:34
  35.4 21.3 %fusion.57 = f32[4,64,7,192]{3,1,2,0:T(8,128)S(1)} fusion(bf16[4,7,27]{2,1,0:T(8,128)(2,1)S(1)} %fusion.56, bf16[4,64,27,64]{3,1,2,0:T(8,128)(2,1)S(1)} %copy.30, bf16[4,27,64,192]{3,2,1,0:T(8,128)(2,1)S(1)} %bitcast.78, pred[4,27]{1,0:T(4,128)(4,1)S(1)} %copy-done.5), kind=kOutput, calls=%fused_computation.11.clone.1 | convolution fusion | flops 1202798592 | bytes 4916820 | tf_op jit(solution)/shard_map/while/body/eval_jaxpr/bsrkc,bkcq->brsq/dot_general | solution.py:35
  62.0 2.7 %gather_fusion = bf16[108,64,192]{2,1,0:T(8,128)(2,1)} fusion(bf16[44,64,192]{2,1,0:T(8,128)(2,1)S(1)} %get-tuple-element.173, s32[1024]{0:T(1024)S(1)} %pad_clamp_fusion.4), kind=kCustom, calls=%fused_computation.clone.1 | custom fusion | bytes 5308848 | tf_op jit(solution)/shard_map/while/body/eval_jaxpr/jit(_take)/gather | solution.py:53
  67.4 3.2 %mul.147 = bf16[4,64,27,64]{3,2,1,0:T(8,128)(2,1)S(1)} reshape(bf16[1,4,64,1728]{3,2,1,0:T(8,128)(2,1)} %constant_dynamic-slice_fusion.2) | data formatting | bytes 1769472 | tf_op jit(solution)/shard_map/while/body/eval_jaxpr/mul | solution.py:34
  72.6 21.3 %fusion.57 = f32[4,64,7,192]{3,1,2,0:T(8,128)S(1)} fusion(bf16[4,7,27]{2,1,0:T(8,128)(2,1)S(1)} %fusion.56, bf16[4,64,27,64]{3,1,2,0:T(8,128)(2,1)S(1)} %copy.30, bf16[4,27,64,192]{3,2,1,0:T(8,128)(2,1)S(1)} %bitcast.78, pred[4,27]{1,0:T(4,128)(4,1)S(1)} %copy-done.5), kind=kOutput, calls=%fused_computation.11.clone.1 | convolution fusion | flops 1202798592 | bytes 4916820 | tf_op jit(solution)/shard_map/while/body/eval_jaxpr/bsrkc,bkcq->brsq/dot_general | solution.py:35
  104.7 3.2 %mul.147 = bf16[4,64,27,64]{3,2,1,0:T(8,128)(2,1)S(1)} reshape(bf16[1,4,64,1728]{3,2,1,0:T(8,128)(2,1)} %constant_dynamic-slice_fusion.2) | data formatting | bytes 1769472 | tf_op jit(solution)/shard_map/while/body/eval_jaxpr/mul | solution.py:34
  109.9 21.3 %fusion.57 = f32[4,64,7,192]{3,1,2,0:T(8,128)S(1)} fusion(bf16[4,7,27]{2,1,0:T(8,128)(2,1)S(1)} %fusion.56, bf16[4,64,27,64]{3,1,2,0:T(8,128)(2,1)S(1)} %copy.30, bf16[4,27,64,192]{3,2,1,0:T(8,128)(2,1)S(1)} %bitcast.78, pred[4,27]{1,0:T(4,128)(4,1)S(1)} %copy-done.5), kind=kOutput, calls=%fused_computation.11.clone.1 | convolution fusion | flops 1202798592 | bytes 4916820 | tf_op jit(solution)/shard_map/while/body/eval_jaxpr/bsrkc,bkcq->brsq/dot_general | solution.py:35
  142.0 3.2 %mul.147 = bf16[4,64,27,64]{3,2,1,0:T(8,128)(2,1)S(1)} reshape(bf16[1,4,64,1728]{3,2,1,0:T(8,128)(2,1)} %constant_dynamic-slice_fusion.2) | data formatting | bytes 1769472 | tf_op jit(solution)/shard_map/while/body/eval_jaxpr/mul | solution.py:34
  147.2 21.3 %fusion.57 = f32[4,64,7,192]{3,1,2,0:T(8,128)S(1)} fusion(bf16[4,7,27]{2,1,0:T(8,128)(2,1)S(1)} %fusion.56, bf16[4,64,27,64]{3,1,2,0:T(8,128)(2,1)S(1)} %copy.30, bf16[4,27,64,192]{3,2,1,0:T(8,128)(2,1)S(1)} %bitcast.78, pred[4,27]{1,0:T(4,128)(4,1)S(1)} %copy-done.5), kind=kOutput, calls=%fused_computation.11.clone.1 | convolution fusion | flops 1202798592 | bytes 4916820 | tf_op jit(solution)/shard_map/while/body/eval_jaxpr/bsrkc,bkcq->brsq/dot_general | solution.py:35
  173.7 3.5 %fusion.47 = (bf16[3,4,64,576]{2,3,1,0:T(8,128)(2,1)}, bf16[3,4,64,576]{2,3,1,0:T(8,128)(2,1)S(1)}) fusion(bf16[4,4,64,576]{2,3,1,0:T(8,128)(2,1)} %get-tuple-element.82), kind=kLoop, calls=%fused_computation.88 | loop fusion | bytes 3538944 | tf_op jit(solution)/shard_map/slice | solution.py:15
  183.2 3.6 %collective-permute-start.3 = (bf16[12,64,576]{2,1,0:T(8,128)(2,1)}, bf16[12,64,576]{2,1,0:T(8,128)(2,1)}, u32[]{:S(2)}, u32[]{:S(2)}) collective-permute-start(bf16[12,64,576]{2,1,0:T(8,128)(2,1)} %bitcast.85), channel_id=1, source_target_pairs={{1,0},{2,1},{3,2},{4,3},{5,4},{6,5},{7,6},{8,7},{9,8},{10,9},{11,1... | collective-permute-start | bytes 2654216 | tf_op jit(solution)/shard_map/ppermute | solution.py:20
  186.8 3.8 %copy.17 = bf16[4,4,64,576]{3,2,1,0:T(8,128)(2,1)} copy(bf16[4,4,64,576]{2,3,1,0:T(8,128)(2,1)} %get-tuple-element.82) | data formatting | bytes 2359296 | tf_op jit(solution)/shard_map/while | solution.py:56
  192.9 21.7 %collective-permute-done.2 = bf16[12,64,576]{2,1,0:T(8,128)(2,1)} collective-permute-done((bf16[12,64,576]{2,1,0:T(8,128)(2,1)}, bf16[12,64,576]{2,1,0:T(8,128)(2,1)}, u32[]{:S(2)}, u32[]{:S(2)}) %collective-permute-start.2) | collective-permute-done | bytes 884768 | tf_op jit(solution)/shard_map/ppermute | solution.py:18
  214.6 10.6 %collective-permute-done.3 = bf16[12,64,576]{2,1,0:T(8,128)(2,1)} collective-permute-done((bf16[12,64,576]{2,1,0:T(8,128)(2,1)}, bf16[12,64,576]{2,1,0:T(8,128)(2,1)}, u32[]{:S(2)}, u32[]{:S(2)}) %collective-permute-start.3) | collective-permute-done | bytes 884768 | tf_op jit(solution)/shard_map/ppermute | solution.py:20
  225.2 3.0 %fusion.21 = f32[2,64,576]{2,1,0:T(8,128)S(1)} fusion(bf16[40,64,64]{1,2,0:T(8,128)(2,1)} %copy.15, bf16[2,40]{1,0:T(2,128)(2,1)S(1)} %compare_convert_fusion.2, bf16[12,64,576]{2,1,0:T(8,128)(2,1)} %collective-permute-done.3, bf16[16,64,576]{2,1,0:T(8,128)(2,1)S(1)} %bitcast.81, bf16[12,64,576]{2,1,0:T(8,128)(2,1)} %collective-permute-done.2), kind=kOutput, calls=%fused_computation.33 | convolution fusion | flops 380764160 | bytes 3571872 | tf_op jit(solution)/shard_map/wbrc,brq->wcq/dot_general | solution.py:76
  228.2 2.8 %fusion.24 = f32[2,64,576]{2,1,0:T(8,128)S(1)} fusion(bf16[40,64,64]{1,2,0:T(8,128)(2,1)S(1)} %copy.19, bf16[2,40]{1,0:T(2,128)(2,1)S(1)} %compare_convert_fusion.1, bf16[12,64,576]{2,1,0:T(8,128)(2,1)} %collective-permute-done.3, bf16[16,64,576]{2,1,0:T(8,128)(2,1)S(1)} %bitcast.82, bf16[12,64,576]{2,1,0:T(8,128)(2,1)} %collective-permute-done.2), kind=kOutput, calls=%fused_computation.34 | convolution fusion | flops 380764160 | bytes 3571872 | tf_op jit(solution)/shard_map/wbrc,brq->wcq/dot_general | solution.py:76
  231.0 2.8 %fusion.27 = f32[2,64,576]{2,1,0:T(8,128)S(1)} fusion(bf16[40,64,64]{1,2,0:T(8,128)(2,1)S(1)} %copy.20, bf16[2,40]{1,0:T(2,128)(2,1)S(1)} %compare_convert_fusion, bf16[12,64,576]{2,1,0:T(8,128)(2,1)} %collective-permute-done.3, bf16[16,64,576]{2,1,0:T(8,128)(2,1)S(1)} %bitcast.83, bf16[12,64,576]{2,1,0:T(8,128)(2,1)} %collective-permute-done.2), kind=kOutput, calls=%fused_computation.35 | convolution fusion | flops 380764160 | bytes 3571872 | tf_op jit(solution)/shard_map/wbrc,brq->wcq/dot_general | solution.py:76
  (108 shorter events, 59.9 us)
Async XLA Ops:
  0.0 9.4 %copy-start = (s32[512]{0:T(512)S(1)}, s32[512]{0:T(512)}, u32[]{:S(2)}) copy-start(s32[512]{0:T(512)} %param.9) | copy-start | bytes 6148
  1.2 18.8 %collective-permute-start = (bf16[14,64,192]{2,1,0:T(8,128)(2,1)S(1)}, bf16[14,64,192]{2,1,0:T(8,128)(2,1)S(1)}, u32[]{:S(2)}, u32[]{:S(2)}) collective-permute-start(bf16[14,64,192]{2,1,0:T(8,128)(2,1)S(1)} %get-tuple-element.106), channel_id=1, source_target_pairs={{0,1},{1,2},{2,3},{3,4},{4,5},{5,6},{6,7},{7,8},{8,9},{9,10},{10,1... | collective-permute-start | bytes 1032200 | tf_op jit(solution)/shard_map/ppermute | solution.py:18
  4.2 20.3 %collective-permute-start.1 = (bf16[14,64,192]{2,1,0:T(8,128)(2,1)S(1)}, bf16[14,64,192]{2,1,0:T(8,128)(2,1)S(1)}, u32[]{:S(2)}, u32[]{:S(2)}) collective-permute-start(bf16[14,64,192]{2,1,0:T(8,128)(2,1)S(1)} %get-tuple-element.105), channel_id=1, source_target_pairs={{1,0},{2,1},{3,2},{4,3},{5,4},{6,5},{7,6},{8,7},{9,8},{10,9},{11,1... | collective-permute-start | bytes 1032200 | tf_op jit(solution)/shard_map/ppermute | solution.py:20
  9.4 4.1 %copy-start.4 = (s32[16,27]{1,0:T(8,128)S(1)}, s32[16,27]{1,0:T(8,128)}, u32[]{:S(2)}) copy-start(s32[16,27]{1,0:T(8,128)} %param.8) | copy-start | bytes 5188
  9.4 10.7 %copy-start.2 = (bf16[16,64,192]{2,1,0:T(8,128)(2,1)S(1)}, bf16[16,64,192]{2,1,0:T(8,128)(2,1)}, u32[]{:S(2)}) copy-start(bf16[16,64,192]{2,1,0:T(8,128)(2,1)} %param.7) | copy-start | bytes 1179652
  33.3 2.0 copy-start.1
  33.4 2.0 copy-start.5
  70.6 2.0 copy-start.1
  70.6 2.0 copy-start.5
  107.9 2.0 copy-start.1
  107.9 2.0 copy-start.5
  145.2 2.0 copy-start.1
  145.2 2.0 copy-start.5
  177.2 9.6 %copy-start.6 = (s32[40]{0:T(128)S(1)}, s32[40]{0:T(128)}, u32[]{:S(2)}) copy-start(s32[40]{0:T(128)} %get-tuple-element.95) | copy-start | bytes 484
  177.2 9.6 %copy-start.8 = (s32[40]{0:T(128)S(1)}, s32[40]{0:T(128)}, u32[]{:S(2)}) copy-start(s32[40]{0:T(128)} %get-tuple-element.109) | copy-start | bytes 484
  177.2 9.6 %copy-start.7 = (s32[40]{0:T(128)S(1)}, s32[40]{0:T(128)}, u32[]{:S(2)}) copy-start(s32[40]{0:T(128)} %get-tuple-element.110) | copy-start | bytes 484
  179.9 34.8 %collective-permute-start.2 = (bf16[12,64,576]{2,1,0:T(8,128)(2,1)}, bf16[12,64,576]{2,1,0:T(8,128)(2,1)}, u32[]{:S(2)}, u32[]{:S(2)}) collective-permute-start(bf16[12,64,576]{2,1,0:T(8,128)(2,1)} %bitcast.84), channel_id=1, source_target_pairs={{0,1},{1,2},{2,3},{3,4},{4,5},{5,6},{6,7},{7,8},{8,9},{9,10},{10,1... | collective-permute-start | bytes 2654216 | tf_op jit(solution)/shard_map/ppermute | solution.py:18
  183.2 42.0 %collective-permute-start.3 = (bf16[12,64,576]{2,1,0:T(8,128)(2,1)}, bf16[12,64,576]{2,1,0:T(8,128)(2,1)}, u32[]{:S(2)}, u32[]{:S(2)}) collective-permute-start(bf16[12,64,576]{2,1,0:T(8,128)(2,1)} %bitcast.85), channel_id=1, source_target_pairs={{1,0},{2,1},{3,2},{4,3},{5,4},{6,5},{7,6},{8,7},{9,8},{10,9},{11,1... | collective-permute-start | bytes 2654216 | tf_op jit(solution)/shard_map/ppermute | solution.py:20
  191.2 34.1 %copy-start.3 = (bf16[4,4,64,576]{3,2,1,0:T(8,128)(2,1)S(1)}, bf16[4,4,64,576]{3,2,1,0:T(8,128)(2,1)}, u32[]{:S(2)}) copy-start(bf16[4,4,64,576]{3,2,1,0:T(8,128)(2,1)} %copy.17) | copy-start | bytes 3538948
where the time goes:
time: 236 us; the launch traced here: 235 us
  matrix products  93.7 us (40%)
  local copies, waits for them, and re-layouts  80.4 us (34%)
  waiting for transfers between devices  42 us (18%)
  starting transfers between devices  11.9 us (5%)
  other arithmetic  6.35 us (3%)
    dot_general x4, matrix products, tile_bands(): jnp.einsum('bsrkc,bkcq->brsq', masked, picked, preferred_element_type=jnp...  85.2 us
    ppermute x2, waiting for transfers between devices, with_halo(): lax.ppermute(tail, axis, [(i, (i + 1) % count) for i in range(count)])  27 us
    mul x8, local copies, waits for them, and re-layouts, tile_bands(): masked = blocks[:, None] * selector[:, :, None, :, None]  15.5 us
    ppermute x2, waiting for transfers between devices, with_halo(): lax.ppermute(head, axis, [((i + 1) % count, i) for i in range(count)])  15 us
    gather x4, local copies, waits for them, and re-layouts, block_bands(): picked = jnp.take(p_ext, local_piece, axis=0)  10.9 us
    dynamic_slice x4, local copies, waits for them, and re-layouts, own_bands(): lax.map(block_bands, (a_tiles.reshape(block_count, 4, tile_size, a_tiles....  8.71 us
    transpose x4, local copies, waits for them, and re-layouts, tile_bands(): jnp.einsum('bsrkc,bkcq->brsq', masked, picked, preferred_element_type=jnp...  8.53 us
    dot_general x3, matrix products, coarse_terms(): jnp.einsum('wbrc,brq->wcq', masked, widened, preferred_element_type=jnp.f...  8.51 us
  transfers between devices with their start and end apart: 4, of which 4 were waited for; matrix products, arithmetic and copies ran while one was open for 6% of the time, Pallas kernels for 0%

commit v1 on v0

v1 whole, which is shorter than its diff:
```python
import functools

import jax
import jax.numpy as jnp
from jax import lax
from jax.experimental import pallas as pl
from jax.experimental.pallas import tpu as pltpu
from jax.sharding import PartitionSpec as P

RATIO = 8
REACH = 14
MESH = pl.DeviceIdType.MESH


def dot(a, b):
    return jnp.dot(a, b, preferred_element_type=jnp.float32)


def galerkin_kernel(
    rows_dev, tile, links, ring, grp, agg, acols, a_hbm, p_hbm, out,
    found, tbl, a2, a_tail, p_own, p_left, p_right, ad, p4, p4t, band, part, got_left, got_right,
    a_sem, p_sem, t_sem, halo_send, halo_recv, part_send, part_recv,
):
    lane = 2 * tile
    halo = REACH
    pairs = (links + 1) // 2
    groups = rows_dev // 2 + halo
    me = lax.axis_index("rows") * grp + lax.axis_index("grp")
    right, left = lax.rem(me + 1, ring), lax.rem(me + ring - 1, ring)

    def device(d):
        return (d // grp, lax.rem(d, grp))

    full = links // 2
    a_copies = [
        pltpu.make_async_copy(
            a_hbm.at[:, :, pl.ds(g * lane, lane)], a2.at[g], a_sem.at[g]
        )
        for g in range(full)
    ]
    a_copies.append(
        pltpu.make_async_copy(
            a_hbm.at[:, :, pl.ds(full * lane, tile)], a_tail, a_sem.at[full]
        )
    )
    p_copy = pltpu.make_async_copy(p_hbm, p_own, p_sem)
    p_copy.start()
    for copy in a_copies:
        copy.start()

    barrier = pltpu.get_barrier_semaphore()
    for neighbour in (left, right):
        pl.semaphore_signal(barrier, inc=1, device_id=device(neighbour), device_id_type=MESH)
    pl.semaphore_wait(barrier, 2)

    to_right = pltpu.make_async_remote_copy(
        p_hbm.at[pl.ds(rows_dev - halo, halo)], p_left,
        halo_send.at[0], halo_recv.at[0], device_id=device(right), device_id_type=MESH,
    )
    to_left = pltpu.make_async_remote_copy(
        p_hbm.at[pl.ds(0, halo)], p_right,
        halo_send.at[1], halo_recv.at[1], device_id=device(left), device_id_type=MESH,
    )
    to_right.start()
    to_left.start()

    total_rows = rows_dev * ring
    first_row = me * rows_dev
    row = lax.broadcasted_iota(jnp.int32, found.shape, 0)
    spot = lax.broadcasted_iota(jnp.int32, found.shape, 1)
    half = spot & 1
    table = (half if links % 2 == 0 else 1 - half) * pairs + links // 2
    for k in range(links):
        at = jnp.broadcast_to(acols[:, k : k + 1], found.shape) - first_row - row + REACH
        at = jnp.where(at < 0, at + total_rows, at)
        at = jnp.where(at >= total_rows, at - total_rows, at) + (row & 1)
        side = half if k % 2 == 0 else 1 - half
        table = jnp.where(at == spot, side * pairs + k // 2, table)
    found[...] = table
    t_copy = pltpu.make_async_copy(found, tbl, t_sem)
    t_copy.start()

    def place(p_ref, count, base):
        def step(r, carry):
            x = p_ref[r]
            own = agg[lax.rem(first_row + total_rows - halo + base + r, total_rows)] & 1
            odd = jnp.full((tile, 4 * tile), own, jnp.int32).astype(jnp.float32).astype(jnp.bfloat16)
            gap = jnp.zeros((tile, tile), jnp.bfloat16)
            low = jnp.concatenate([x, gap], axis=1)
            high = jnp.concatenate([gap, x], axis=1)
            p4[pl.ds(pl.multiple_of((base + r) * tile, tile), tile), :] = (
                low * (jnp.bfloat16(1) - odd) + high * odd
            )
            return carry

        lax.fori_loop(0, count, step, 0)

    p_copy.wait()
    place(p_own, rows_dev, halo)
    p4t[...] = p4[halo * tile : (halo + rows_dev) * tile, :].T

    def swap(g):
        def step(r, carry):
            x = a2[g, r]
            a2[pairs + g, r] = jnp.concatenate([x[:, tile:], x[:, :tile]], axis=1)
            return carry

        lax.fori_loop(0, rows_dev, step, 0)

    for g in range(full):
        a_copies[g].wait()
        swap(g)
    a_copies[full].wait()

    def swap_tail(r, carry):
        x, gap = a_tail[r], jnp.zeros((tile, tile), jnp.bfloat16)
        a2[full, r] = jnp.concatenate([x, gap], axis=1)
        a2[pairs + full, r] = jnp.concatenate([gap, x], axis=1)
        return carry

    lax.fori_loop(0, rows_dev, swap_tail, 0)
    t_copy.wait()

    span = REACH + 1
    first_half = lax.broadcasted_iota(jnp.int32, (tile, lane), 1) < tile

    def gather(r2, carry):
        for parity in range(2):
            r = 2 * r2 + parity
            rows = pl.ds(pl.multiple_of(r * tile, tile), tile)
            for g in range(span):
                x0 = a2[tbl[r, 2 * g], r]
                x1 = a2[tbl[r, 2 * g + 1], r]
                ad[rows, pl.ds(pl.multiple_of((r2 + g) * lane, lane), lane)] = jnp.where(
                    first_half, x0, x1
                )
        return carry

    lax.fori_loop(0, rows_dev // 2, gather, 0)

    empty = jnp.zeros((2 * tile, lane), jnp.bfloat16)
    for r2 in range(rows_dev // 2):
        for g in range(groups):
            if g < r2 or g >= r2 + span:
                ad[r2 * lane : (r2 + 1) * lane, g * lane : (g + 1) * lane] = empty

    chunk = 4 * tile
    k_left, k_own, k_all = halo * tile, (halo + rows_dev) * tile, (2 * halo + rows_dev) * tile
    own_sum = part

    def own_part(c, carry):
        rows = pl.ds(pl.multiple_of(c * chunk, chunk), chunk)
        own_sum[rows, :] = dot(ad[rows, k_left:k_own], p4[k_left:k_own, :])
        return carry

    lax.fori_loop(0, rows_dev // 4, own_part, 0)

    to_right.wait()
    place(p_left, halo, 0)
    to_left.wait()
    place(p_right, halo, halo + rows_dev)

    def ends(c, carry):
        rows = pl.ds(pl.multiple_of(c * chunk, chunk), chunk)
        low = dot(ad[rows, 0:k_left], p4[0:k_left, :])
        high = dot(ad[rows, k_own:k_all], p4[k_own:k_all, :])
        mid = own_sum[rows, :]
        band[rows, 0:lane] = low[:, :lane].astype(jnp.bfloat16)
        band[rows, lane : 2 * lane] = (low[:, lane:] + mid[:, :lane]).astype(jnp.bfloat16)
        band[rows, 2 * lane : 3 * lane] = (high[:, :lane] + mid[:, lane:]).astype(jnp.bfloat16)
        band[rows, 3 * lane : 4 * lane] = high[:, lane:].astype(jnp.bfloat16)
        return carry

    lax.fori_loop(0, rows_dev // 4, ends, 0)

    send_left, send_right = got_left.at[1], got_right.at[1]
    outer = dot(p4t[0:tile, :], band[...])
    send_left[...] = outer.astype(jnp.bfloat16)
    part_left = pltpu.make_async_remote_copy(
        send_left, got_right.at[0],
        part_send.at[0], part_recv.at[0], device_id=device(left), device_id_type=MESH,
    )
    part_left.start()
    outer = dot(p4t[3 * tile : 4 * tile, :], band[...])
    send_right[...] = outer.astype(jnp.bfloat16)
    part_right = pltpu.make_async_remote_copy(
        send_right, got_left.at[0],
        part_send.at[1], part_recv.at[1], device_id=device(right), device_id_type=MESH,
    )
    part_right.start()
    inner = dot(p4t[tile : 3 * tile, :], band[...])
    even, odd = inner[:tile], inner[tile:]

    edge = jnp.zeros((tile, lane), jnp.float32)
    even = jnp.concatenate([edge, even, jnp.zeros((tile, tile), jnp.float32)], axis=1)
    part_right.wait()
    from_left = got_left[0].astype(jnp.float32)
    out[0] = even + jnp.concatenate([from_left, jnp.zeros((tile, 3 * tile), jnp.float32)], axis=1)
    part_left.wait()
    from_right = got_right[0].astype(jnp.float32)
    odd = jnp.concatenate([odd, edge], axis=1) + jnp.concatenate([edge, from_right], axis=1)
    out[1] = jnp.concatenate([jnp.zeros((tile, tile), jnp.float32), odd], axis=1)


def shards(a_tiles, p_tiles, acols, agg):
    rows_dev, tile, width = a_tiles.shape
    links = width // tile
    grp = lax.axis_size("grp")
    ring = lax.axis_size("rows") * grp
    halo = REACH
    bf16, f32 = jnp.bfloat16, jnp.float32
    pairs = (links + 1) // 2
    lane = 2 * tile
    n_all = rows_dev + 2 * halo
    return pl.pallas_call(
        functools.partial(galerkin_kernel, rows_dev, tile, links, ring, grp),
        out_shape=jax.ShapeDtypeStruct((rows_dev // RATIO, tile, 11 * tile), f32),
        in_specs=[
            pl.BlockSpec(memory_space=pltpu.SMEM),
            pl.BlockSpec(memory_space=pltpu.VMEM),
            pl.BlockSpec(memory_space=pl.ANY),
            pl.BlockSpec(memory_space=pl.ANY),
        ],
        out_specs=pl.BlockSpec(memory_space=pltpu.VMEM),
        scratch_shapes=[
            pltpu.VMEM((rows_dev, lane), jnp.int32),
            pltpu.SMEM((rows_dev, lane), jnp.int32),
            pltpu.VMEM((2 * pairs, rows_dev, tile, lane), bf16),
            pltpu.VMEM((rows_dev, tile, tile), bf16),
            pltpu.VMEM((rows_dev, tile, 3 * tile), bf16),
            pltpu.VMEM((halo, tile, 3 * tile), bf16),
            pltpu.VMEM((halo, tile, 3 * tile), bf16),
            pltpu.VMEM((rows_dev * tile, n_all * tile), bf16),
            pltpu.VMEM((n_all * tile, 4 * tile), bf16),
            pltpu.VMEM((4 * tile, rows_dev * tile), bf16),
            pltpu.VMEM((rows_dev * tile, 8 * tile), bf16),
            pltpu.VMEM((rows_dev * tile, 4 * tile), f32),
            pltpu.VMEM((2, tile, 8 * tile), bf16),
            pltpu.VMEM((2, tile, 8 * tile), bf16),
            pltpu.SemaphoreType.DMA((pairs,)),
            pltpu.SemaphoreType.DMA,
            pltpu.SemaphoreType.DMA,
            pltpu.SemaphoreType.DMA((2,)),
            pltpu.SemaphoreType.DMA((2,)),
            pltpu.SemaphoreType.DMA((2,)),
            pltpu.SemaphoreType.DMA((2,)),
        ],
        compiler_params=pltpu.CompilerParams(
            collective_id=0, has_side_effects=True, vmem_limit_bytes=60 * 2**20
        ),
    )(agg, acols, a_tiles, p_tiles)


def solution(mesh):
    return jax.shard_map(
        shards,
        mesh=mesh,
        in_specs=(
            P(("rows", "grp"), None, None),
            P(("rows", "grp"), None, None),
            P(("rows", "grp"), None),
            P(),
        ),
        out_specs=P(("rows", "grp"), None, None),
        check_vma=False,
    )
```

time: 236 us -> 40.1 us (0.17)
  matrix products: 93.7 us -> 0 us
  local copies, waits for them, and re-layouts: 80.4 us -> 1.77 us
  waiting for transfers between devices: 42 us -> 0 us
  Pallas kernels: 0 us -> 38.1 us
  starting transfers between devices: 11.9 us -> 0 us
  other arithmetic: 6.35 us -> 0 us
    dot_general x7 -> x0, matrix products: 93.7 us -> none  [the longest x4 85.2 us: tile_bands(): jnp.einsum('bsrkc,bkcq->brsq', masked, picked, preferred_element_type=jnp...]
    ppermute x4 -> x0, waiting for transfers between devices: 42 us -> none  [the longest x2 27 us: with_halo(): lax.ppermute(tail, axis, [(i, (i + 1) % count) for i in range(count)])]
    pallas_call x0 -> x1, Pallas kernels: none -> 38.1 us  [shards(): pl.pallas_call(functools.partial(galerkin_kernel, rows_dev, tile, links,...]
    mul x8 -> x0, local copies, waits for them, and re-layouts: 15.5 us -> none  [tile_bands(): masked = blocks[:, None] * selector[:, :, None, :, None]]
    gather x7 -> x0, local copies, waits for them, and re-layouts: 14.9 us -> none  [the longest x4 10.9 us: block_bands(): picked = jnp.take(p_ext, local_piece, axis=0)]
    ppermute x4 -> x0, starting transfers between devices: 11.9 us -> none  [the longest x2 7.08 us: with_halo(): lax.ppermute(head, axis, [((i + 1) % count, i) for i in range(count)])]
    slice x8 -> x0, local copies, waits for them, and re-layouts: 11.3 us -> none  [the longest x2 6.16 us: with_halo(): lax.slice_in_dim(cells, cells.shape[dim] - width, cells.shape[dim], axis=...]
    dynamic_slice x5 -> x0, local copies, waits for them, and re-layouts: 9.46 us -> none  [the longest x4 8.71 us: own_bands(): lax.map(block_bands, (a_tiles.reshape(block_count, 4, tile_size, a_tiles....]
  transfers between devices with their start and end apart: 4 -> 0, of which waited for: 4 -> 0; matrix products, arithmetic and copies ran while one was open for 6% -> 0% of each run, Pallas kernels for 0% -> 0%
where the time goes in v1:
time: 40.1 us; the launch traced here: 39.8 us
  Pallas kernels  38.1 us (95%)
  local copies, waits for them, and re-layouts  1.77 us (4%)
    pallas_call x1, Pallas kernels, shards(): pl.pallas_call(functools.partial(galerkin_kernel, rows_dev, tile, links,...  38.1 us
    unnamed x1, local copies, waits for them, and re-layouts  1.77 us

profile of v1, /device:TPU:0, one launch (start us, length us, event | category | flops | bytes accessed | tf_op | source)
XLA Modules:
  0.0 39.8 jit_solution(4139244480300893553)
XLA Ops:
  0.0 38.1 %shard_map.46 = f32[2,64,704]{2,1,0:T(8,128)} custom-call(s32[512]{0:T(512)} %agg.1, s32[16,27]{1,0:T(8,128)} %acols.1, bf16[16,64,1728]{2,1,0:T(8,128)(2,1)} %a_hbm.1, bf16[16,64,192]{2,1,0:T(8,128)(2,1)} %p_hbm.1), custom_call_target="tpu_custom_call" | custom-call | tf_op jit(solution)/shard_map/pallas_call | solution.py:215
  38.1 1.8 %copy.6 = f32[2,64,704]{2,1,0:T(8,128)} copy(f32[2,64,704]{2,1,0:T(8,128)} %shard_map.46) | data formatting | bytes 720896

commit v2 on v1

--- a/solution.py
+++ b/solution.py
@@ -18,7 +18,7 @@
 
 def galerkin_kernel(
     rows_dev, tile, links, ring, grp, agg, acols, a_hbm, p_hbm, out,
-    found, tbl, a2, a_tail, p_own, p_left, p_right, ad, p4, p4t, band, part, got_left, got_right,
+    found, tbl, a2, a_tail, p_own, packed, near, ad, p4, p4t, band, part, got_left, got_right,
     a_sem, p_sem, t_sem, halo_send, halo_recv, part_send, part_recv,
 ):
     lane = 2 * tile
@@ -49,20 +49,51 @@
         copy.start()
 
     barrier = pltpu.get_barrier_semaphore()
-    for neighbour in (left, right):
-        pl.semaphore_signal(barrier, inc=1, device_id=device(neighbour), device_id_type=MESH)
-    pl.semaphore_wait(barrier, 2)
-
-    to_right = pltpu.make_async_remote_copy(
-        p_hbm.at[pl.ds(rows_dev - halo, halo)], p_left,
-        halo_send.at[0], halo_recv.at[0], device_id=device(right), device_id_type=MESH,
-    )
-    to_left = pltpu.make_async_remote_copy(
-        p_hbm.at[pl.ds(0, halo)], p_right,
-        halo_send.at[1], halo_recv.at[1], device_id=device(left), device_id_type=MESH,
-    )
-    to_right.start()
-    to_left.start()
+    for step in (1, 2, ring - 2, ring - 1):
+        pl.semaphore_signal(
+            barrier, inc=1, device_id=device(lax.rem(me + step, ring)), device_id_type=MESH
+        )
+
+    p_copy.wait()
+    for r in range(rows_dev):
+        x = p_own[r]
+        packed[r, :tile] = x[:, :lane]
+        packed[r, tile:] = jnp.concatenate([x[: tile // 2, lane:], x[tile // 2 :, lane:]], axis=1)
+    pl.semaphore_wait(barrier, 4)
+
+    spot4 = lax.rem(me, 4)
+    core = spot4 // 2
+    is_inner = (spot4 == 1) | (spot4 == 2)
+    is_outer = (spot4 == 0) | (spot4 == 3)
+    mate = lax.rem(me + 2 + ring - 4 * core, ring)
+    mid, spare = rows_dev // 2, rows_dev - halo
+
+    def send(src, side, start, count, sem, arrival, target):
+        return pltpu.make_async_remote_copy(
+            src.at[pl.ds(start, count)], near.at[side, pl.ds(start, count)],
+            halo_send.at[sem], halo_recv.at[arrival],
+            device_id=device(target), device_id_type=MESH,
+        )
+
+    to_right = send(packed, 0, spare, halo, 0, 2, right)
+    to_left = send(packed, 1, 0, halo, 1, 2, left)
+    half_low = send(packed, 1, 0, mid, 0, 0, left)
+    half_high = send(packed, 0, mid, mid, 1, 0, right)
+    got_half = near.at[1 - core]
+    swap_half = send(got_half, core, mid * core, mid, 2, 1, mate)
+    in_half = send(packed, 1 - core, mid * core, mid, 2, 0, mate)
+    in_swap = send(packed, 1 - core, mid * (1 - core), mid, 2, 1, mate)
+    in_full = send(packed, core, spare * (1 - core), halo, 2, 2, mate)
+
+    @pl.when(is_inner)
+    def _():
+        half_low.start()
+        half_high.start()
+
+    @pl.when(is_outer)
+    def _():
+        to_right.start()
+        to_left.start()
 
     total_rows = rows_dev * ring
     first_row = me * rows_dev
@@ -80,45 +111,43 @@
     t_copy = pltpu.make_async_copy(found, tbl, t_sem)
     t_copy.start()
 
-    def place(p_ref, count, base):
-        def step(r, carry):
-            x = p_ref[r]
+    low_half = lax.broadcasted_iota(jnp.int32, (tile, lane), 1) < tile
+
+    def place(p_ref, from_row, count, base):
+        nothing = jnp.zeros((tile, lane), jnp.bfloat16)
+        for r in range(count):
+            x, y = p_ref[from_row + r, :tile], p_ref[from_row + r, tile:]
+            turned = pltpu.roll(y, tile, 1)
+            rest_low = jnp.concatenate([y, turned], axis=0)
+            rest_high = jnp.concatenate([turned, y], axis=0)
+            x_turned = pltpu.roll(x, tile, 1)
             own = agg[lax.rem(first_row + total_rows - halo + base + r, total_rows)] & 1
-            odd = jnp.full((tile, 4 * tile), own, jnp.int32).astype(jnp.float32).astype(jnp.bfloat16)
-            gap = jnp.zeros((tile, tile), jnp.bfloat16)
-            low = jnp.concatenate([x, gap], axis=1)
-            high = jnp.concatenate([gap, x], axis=1)
-            p4[pl.ds(pl.multiple_of((base + r) * tile, tile), tile), :] = (
-                low * (jnp.bfloat16(1) - odd) + high * odd
+            odd = jnp.full((tile, lane), own, jnp.int32).astype(jnp.float32).astype(jnp.bfloat16)
+            even = jnp.bfloat16(1) - odd
+            rows = slice((base + r) * tile, (base + r + 1) * tile)
+            p4[rows, :lane] = x * even + jnp.where(low_half, nothing, x_turned) * odd
+            p4[rows, lane:] = (
+                jnp.where(low_half, rest_low, nothing) * even
+                + jnp.where(low_half, x_turned, rest_high) * odd
             )
-            return carry
-
-        lax.fori_loop(0, count, step, 0)
-
-    p_copy.wait()
-    place(p_own, rows_dev, halo)
+
+    place(packed, 0, rows_dev, halo)
     p4t[...] = p4[halo * tile : (halo + rows_dev) * tile, :].T
 
-    def swap(g):
-        def step(r, carry):
-            x = a2[g, r]
-            a2[pairs + g, r] = jnp.concatenate([x[:, tile:], x[:, :tile]], axis=1)
-            return carry
-
-        lax.fori_loop(0, rows_dev, step, 0)
-
-    for g in range(full):
-        a_copies[g].wait()
-        swap(g)
-    a_copies[full].wait()
-
-    def swap_tail(r, carry):
-        x, gap = a_tail[r], jnp.zeros((tile, tile), jnp.bfloat16)
+    for copy in a_copies:
+        copy.wait()
+    gap = jnp.zeros((tile, tile), jnp.bfloat16)
+    for r in range(rows_dev):
+        x = a_tail[r]
         a2[full, r] = jnp.concatenate([x, gap], axis=1)
         a2[pairs + full, r] = jnp.concatenate([gap, x], axis=1)
+
+    def swap(g, carry):
+        for r in range(rows_dev):
+            a2[pairs + g, r] = pltpu.roll(a2[g, r], tile, 1)
         return carry
 
-    lax.fori_loop(0, rows_dev, swap_tail, 0)
+    lax.fori_loop(0, full, swap, 0)
     t_copy.wait()
 
     span = REACH + 1
@@ -155,10 +184,12 @@
 
     lax.fori_loop(0, rows_dev // 4, own_part, 0)
 
-    to_right.wait()
-    place(p_left, halo, 0)
-    to_left.wait()
-    place(p_right, halo, halo + rows_dev)
+    in_half.wait_recv()
+    swap_half.start()
+    in_full.wait_recv()
+    in_swap.wait_recv()
+    place(near.at[0], spare, halo, 0)
+    place(near.at[1], 0, halo, halo + rows_dev)
 
     def ends(c, carry):
         rows = pl.ds(pl.multiple_of(c * chunk, chunk), chunk)
@@ -200,6 +231,18 @@
     from_right = got_right[0].astype(jnp.float32)
     odd = jnp.concatenate([odd, edge], axis=1) + jnp.concatenate([edge, from_right], axis=1)
     out[1] = jnp.concatenate([jnp.zeros((tile, tile), jnp.float32), odd], axis=1)
+
+    swap_half.wait_send()
+
+    @pl.when(is_inner)
+    def _():
+        half_low.wait_send()
+        half_high.wait_send()
+
+    @pl.when(is_outer)
+    def _():
+        to_right.wait_send()
+        to_left.wait_send()
 
 
 def shards(a_tiles, p_tiles, acols, agg):
@@ -228,8 +271,8 @@
             pltpu.VMEM((2 * pairs, rows_dev, tile, lane), bf16),
             pltpu.VMEM((rows_dev, tile, tile), bf16),
             pltpu.VMEM((rows_dev, tile, 3 * tile), bf16),
-            pltpu.VMEM((halo, tile, 3 * tile), bf16),
-            pltpu.VMEM((halo, tile, 3 * tile), bf16),
+            pltpu.VMEM((rows_dev, 3 * tile // 2, lane), bf16),
+            pltpu.VMEM((2, rows_dev, 3 * tile // 2, lane), bf16),
             pltpu.VMEM((rows_dev * tile, n_all * tile), bf16),
             pltpu.VMEM((n_all * tile, 4 * tile), bf16),
             pltpu.VMEM((4 * tile, rows_dev * tile), bf16),
@@ -240,13 +283,13 @@
             pltpu.SemaphoreType.DMA((pairs,)),
             pltpu.SemaphoreType.DMA,
             pltpu.SemaphoreType.DMA,
-            pltpu.SemaphoreType.DMA((2,)),
-            pltpu.SemaphoreType.DMA((2,)),
+            pltpu.SemaphoreType.DMA((3,)),
+            pltpu.SemaphoreType.DMA((3,)),
             pltpu.SemaphoreType.DMA((2,)),
             pltpu.SemaphoreType.DMA((2,)),
         ],
         compiler_params=pltpu.CompilerParams(
-            collective_id=0, has_side_effects=True, vmem_limit_bytes=60 * 2**20
+            collective_id=0, has_side_effects=True, vmem_limit_bytes=58 * 2**20
         ),
     )(agg, acols, a_tiles, p_tiles)
 

time: 40.1 us -> 27.2 us (0.68)
  the two profiles are of different devices: /device:TPU:0 before, /device:TPU:25 now
where the time goes in v2:
time: 27.2 us; the launch traced here: 27 us
  Pallas kernels  25.2 us (93%)
  local copies, waits for them, and re-layouts  1.77 us (7%)
    pallas_call x1, Pallas kernels, shards(): pl.pallas_call(functools.partial(galerkin_kernel, rows_dev, tile, links,...  25.2 us
    unnamed x1, local copies, waits for them, and re-layouts  1.77 us

profile of v2, /device:TPU:25, one launch (start us, length us, event | category | flops | bytes accessed | tf_op | source)
XLA Modules:
  0.0 27.0 jit_solution(17216222157991983769)
XLA Ops:
  0.0 25.2 %shard_map.46 = f32[2,64,704]{2,1,0:T(8,128)} custom-call(s32[512]{0:T(512)} %agg.1, s32[16,27]{1,0:T(8,128)} %acols.1, bf16[16,64,1728]{2,1,0:T(8,128)(2,1)} %a_hbm.1, bf16[16,64,192]{2,1,0:T(8,128)(2,1)} %p_hbm.1), custom_call_target="tpu_custom_call" | custom-call | tf_op jit(solution)/shard_map/pallas_call | solution.py:258
  25.2 1.8 %copy.6 = f32[2,64,704]{2,1,0:T(8,128)} copy(f32[2,64,704]{2,1,0:T(8,128)} %shard_map.46) | data formatting | bytes 720896

commit v3 on v2

--- a/solution.py
+++ b/solution.py
@@ -49,23 +49,20 @@
         copy.start()
 
     barrier = pltpu.get_barrier_semaphore()
-    for step in (1, 2, ring - 2, ring - 1):
-        pl.semaphore_signal(
-            barrier, inc=1, device_id=device(lax.rem(me + step, ring)), device_id_type=MESH
-        )
+    spot4 = lax.rem(me, 4)
+    core = spot4 // 2
+    mate = lax.rem(me + 2 + ring - 4 * core, ring)
+    for partner in (left, right, mate):
+        pl.semaphore_signal(barrier, inc=1, device_id=device(partner), device_id_type=MESH)
 
     p_copy.wait()
     for r in range(rows_dev):
         x = p_own[r]
         packed[r, :tile] = x[:, :lane]
         packed[r, tile:] = jnp.concatenate([x[: tile // 2, lane:], x[tile // 2 :, lane:]], axis=1)
-    pl.semaphore_wait(barrier, 4)
-
-    spot4 = lax.rem(me, 4)
-    core = spot4 // 2
+    pl.semaphore_wait(barrier, 3)
+
     is_inner = (spot4 == 1) | (spot4 == 2)
-    is_outer = (spot4 == 0) | (spot4 == 3)
-    mate = lax.rem(me + 2 + ring - 4 * core, ring)
     mid, spare = rows_dev // 2, rows_dev - halo
 
     def send(src, side, start, count, sem, arrival, target):
@@ -90,7 +87,12 @@
         half_low.start()
         half_high.start()
 
-    @pl.when(is_outer)
+    @pl.when(spot4 == 0)
+    def _():
+        to_left.start()
+        to_right.start()
+
+    @pl.when(spot4 == 3)
     def _():
         to_right.start()
         to_left.start()
@@ -239,7 +241,7 @@
         half_low.wait_send()
         half_high.wait_send()
 
-    @pl.when(is_outer)
+    @pl.when((spot4 == 0) | (spot4 == 3))
     def _():
         to_right.wait_send()
         to_left.wait_send()
@@ -289,7 +291,7 @@
             pltpu.SemaphoreType.DMA((2,)),
         ],
         compiler_params=pltpu.CompilerParams(
-            collective_id=0, has_side_effects=True, vmem_limit_bytes=58 * 2**20
+            collective_id=0, has_side_effects=True, vmem_limit_bytes=52 * 2**20
         ),
     )(agg, acols, a_tiles, p_tiles)
 

time: 27.2 us -> 26.7 us (0.982)
  the two profiles are of different devices: /device:TPU:25 before, /device:TPU:0 now
where the time goes in v3:
time: 26.7 us; the launch traced here: 26.4 us
  Pallas kernels  23.3 us (87%)
  local copies, waits for them, and re-layouts  3.17 us (12%)
    pallas_call x1, Pallas kernels, shards(): pl.pallas_call(functools.partial(galerkin_kernel, rows_dev, tile, links,...  23.3 us
    unnamed x7, local copies, waits for them, and re-layouts  3.17 us

profile of v3, /device:TPU:0, one launch (start us, length us, event | category | flops | bytes accessed | tf_op | source)
XLA Modules:
  0.0 26.4 jit_solution(16860366387585977385)
XLA Ops:
  0.0 0.0 copy-start
  0.0 1.0 %copy-done = bf16[16,64,192]{2,1,0:T(8,128)(2,1)S(1)} copy-done((bf16[16,64,192]{2,1,0:T(8,128)(2,1)S(1)}, bf16[16,64,192]{2,1,0:T(8,128)(2,1)}, u32[]{:S(2)}) %copy-start) | copy-done | bytes 393240
  1.0 0.0 copy-start.1
  1.0 0.7 %copy-done.1 = s32[16,27]{1,0:T(8,128)S(1)} copy-done((s32[16,27]{1,0:T(8,128)S(1)}, s32[16,27]{1,0:T(8,128)}, u32[]{:S(2)}) %copy-start.1) | copy-done | bytes 1752
  1.7 0.0 copy-start.2
  1.7 0.7 %copy-done.2 = s32[512]{0:T(512)S(1)} copy-done((s32[512]{0:T(512)S(1)}, s32[512]{0:T(512)}, u32[]{:S(2)}) %copy-start.2) | copy-done | bytes 2072
  2.4 23.3 %shard_map.46 = f32[2,64,704]{2,1,0:T(8,128)S(1)} custom-call(s32[512]{0:T(512)S(1)} %copy-done.2, s32[16,27]{1,0:T(8,128)S(1)} %copy-done.1, bf16[16,64,1728]{2,1,0:T(8,128)(2,1)} %a_hbm.1, bf16[16,64,192]{2,1,0:T(8,128)(2,1)S(1)} %copy-done), custom_call_target="tpu_custom_call" | custom-call | tf_op jit(solution)/shard_map/pallas_call | solution.py:260
  25.7 0.7 %copy.6 = f32[2,64,704]{2,1,0:T(8,128)} copy(f32[2,64,704]{2,1,0:T(8,128)S(1)} %shard_map.46) | data formatting | bytes 720896
Async XLA Ops:
  0.0 1.0 %copy-start = (bf16[16,64,192]{2,1,0:T(8,128)(2,1)S(1)}, bf16[16,64,192]{2,1,0:T(8,128)(2,1)}, u32[]{:S(2)}) copy-start(bf16[16,64,192]{2,1,0:T(8,128)(2,1)} %p_hbm.1) | copy-start | bytes 1179652
  1.0 0.7 %copy-start.1 = (s32[16,27]{1,0:T(8,128)S(1)}, s32[16,27]{1,0:T(8,128)}, u32[]{:S(2)}) copy-start(s32[16,27]{1,0:T(8,128)} %acols.1) | copy-start | bytes 5188
  1.7 0.7 %copy-start.2 = (s32[512]{0:T(512)S(1)}, s32[512]{0:T(512)}, u32[]{:S(2)}) copy-start(s32[512]{0:T(512)} %agg.1) | copy-start | bytes 6148
